TPU v7x, 32 devices: a whole 2x2x4 slice. The times are simulated.
32 devices in a mesh: rep: 4 (over z), fsdp: 8 (over y, x, core).
Axes of the slice: x: 2, y: 2, z: 4, core: 2. Of those that a mesh axis runs over, the one named last changes fastest.
Arguments:
- layer_input: bfloat16 [16, 1024, 768], P('rep', 'fsdp'), may hold values from -40 to 40
- positions: int32 [16, 1024], P('rep', 'fsdp'), may hold values from 0 to 1023, as said below
- cotangent: bfloat16 [16, 1024, 768], P('rep', 'fsdp'), may hold values from -6 to 6
- w_qkv: bfloat16 [768, 2304], P('fsdp'), may hold values from -4 to 4
- w_out: bfloat16 [768, 768], P('fsdp'), may hold values from -1.75 to 1.75
- w_up: bfloat16 [768, 3072], P('fsdp'), may hold values from -0.21875 to 0.21875
- w_down: bfloat16 [768, 3072], P('fsdp'), may hold values from -0.109375 to 0.109375
- ln1_gain: bfloat16 [768], P('fsdp'), may hold values from 0.5 to 1.5
- ln1_bias: bfloat16 [768], P('fsdp'), may hold values from -1.5 to 1.5
- ln2_gain: bfloat16 [768], P('fsdp'), may hold values from 0.5 to 1.5
- ln2_bias: bfloat16 [768], P('fsdp'), may hold values from -1.5 to 1.5
- qkv_bias: bfloat16 [2304], P('fsdp'), may hold values from -2.5 to 2.5
- out_bias: bfloat16 [768], P('fsdp'), may hold values from -2.5 to 2.5
- up_bias: bfloat16 [3072], P('fsdp'), may hold values from -2.5 to 2.5
- down_bias: bfloat16 [768], P('fsdp'), may hold values from -2.5 to 2.5
Outputs:
- output: bfloat16 [16, 1024, 768], P('rep', 'fsdp')
- grad_input: bfloat16 [16, 1024, 768], P('rep', 'fsdp')
- grad_w_qkv: float32 [768, 2304], P('fsdp')
- grad_w_out: float32 [768, 768], P('fsdp')
- grad_w_up: float32 [768, 3072], P('fsdp')
- grad_w_down: float32 [768, 3072], P('fsdp')
- grad_ln1_gain: float32 [768], P('fsdp')
- grad_ln1_bias: float32 [768], P('fsdp')
- grad_ln2_gain: float32 [768], P('fsdp')
- grad_ln2_bias: float32 [768], P('fsdp')
- grad_qkv_bias: float32 [2304], P('fsdp')
- grad_out_bias: float32 [768], P('fsdp')
- grad_up_bias: float32 [3072], P('fsdp')
- grad_down_bias: float32 [768], P('fsdp')
Inputs may be any that keep to these rules, and one draw needn't show every extreme that they name: positions[s, 0] is 0, and each later positions[s, t] is either 0 or positions[s, t - 1] + 1; sequence 0 is one document of 1024 tokens.
All inputs are finite; a program needn't handle non-finite values.
Results may differ from a plain program's by a relative error of at most 0.0093.
Values may be sent and summed in bfloat16 or wider, within the bound.
No kernel may reach another device: no remote copies, remote signals or barrier semaphores. Data moves between devices by JAX's collectives and lax.ppermute only.
A program may use at most 320 MiB of HBM per device.

v0:
```python
import jax
import jax.numpy as jnp
from jax import lax
from jax.sharding import PartitionSpec as P

H = 12
HD = 64
ROT = 16
EPS = 1e-05
NEG = -1e30


def norm_rows(values, gain, shift):
    mean = jnp.mean(values, axis=-1, keepdims=True)
    centred = values - mean
    spread = jnp.mean(centred * centred, axis=-1, keepdims=True)
    return centred * lax.rsqrt(spread + EPS) * gain + shift


def rotate(values, cosine, sine):
    half = ROT // 2
    head = values[..., :ROT]
    turned = jnp.concatenate([-head[..., half:], head[..., :half]], axis=-1)
    return jnp.concatenate([head * cosine + turned * sine, values[..., ROT:]], axis=-1)


def angles(positions):
    inverse = 10000.0 ** (-jnp.arange(0, ROT, 2, dtype=jnp.float32) / ROT)
    phase = positions.astype(jnp.float32)[..., None] * inverse
    phase = jnp.concatenate([phase, phase], axis=-1)[..., None, :]
    return (jnp.cos(phase), jnp.sin(phase))


def on_device(
    layer_input,
    positions,
    cotangent,
    w_qkv,
    w_out,
    w_up,
    w_down,
    ln1_gain,
    ln1_bias,
    ln2_gain,
    ln2_bias,
    qkv_bias,
    out_bias,
    up_bias,
    down_bias,
):
    seq_count, span_len, width = layer_input.shape
    shard_count = lax.axis_size("fsdp")
    shard_index = lax.axis_index("fsdp")
    row_count = seq_count * span_len
    qkv_cols = w_qkv.shape[1]
    hidden_cols = w_up.shape[1]
    vectors = (
        lax.all_gather(ln1_gain, "fsdp", axis=0, tiled=True),
        lax.all_gather(ln1_bias, "fsdp", axis=0, tiled=True),
        lax.all_gather(ln2_gain, "fsdp", axis=0, tiled=True),
        lax.all_gather(ln2_bias, "fsdp", axis=0, tiled=True),
        lax.all_gather(qkv_bias, "fsdp", axis=0, tiled=True),
        lax.all_gather(out_bias, "fsdp", axis=0, tiled=True),
        lax.all_gather(up_bias, "fsdp", axis=0, tiled=True),
        lax.all_gather(down_bias, "fsdp", axis=0, tiled=True),
    )
    gain_one, shift_one, gain_two, shift_two, bias_qkv, bias_out, bias_up, bias_down = [
        v.astype(jnp.float32) for v in vectors
    ]
    source = layer_input.reshape(row_count, width).astype(jnp.float32)
    normed_one, pull_one = jax.vjp(norm_rows, source, gain_one, shift_one)
    normed_two, pull_two = jax.vjp(norm_rows, source, gain_two, shift_two)
    input_one = normed_one.astype(jnp.bfloat16)
    input_two = normed_two.astype(jnp.bfloat16)
    pieces = (
        lax.all_gather(w_qkv, "fsdp", axis=0, tiled=True),
        lax.all_gather(w_up, "fsdp", axis=0, tiled=True),
    )
    count = pieces[0].shape[0]
    qkv_sum = jnp.dot(input_one, pieces[0], preferred_element_type=jnp.float32)
    up_sum = jnp.dot(input_two, pieces[1], preferred_element_type=jnp.float32)
    qkv_full = qkv_sum + bias_qkv
    up_full = up_sum + bias_up
    cosine, sine = angles(positions)

    def turn_all(packed):
        shaped = packed.reshape(seq_count, span_len, 3, H, HD)
        return (
            rotate(shaped[:, :, 0], cosine, sine),
            rotate(shaped[:, :, 1], cosine, sine),
            shaped[:, :, 2],
        )

    turned, pull_turn = jax.vjp(turn_all, qkv_full)
    query_low = turned[0].astype(jnp.bfloat16)
    key_low = turned[1].astype(jnp.bfloat16)
    value_low = turned[2].astype(jnp.bfloat16)
    key_flat = key_low.reshape(seq_count, span_len, width)
    value_flat = value_low.reshape(seq_count, span_len, width)
    query_index = shard_index * span_len + jnp.arange(span_len, dtype=jnp.int32)
    first_seen = query_index[None, :] - positions

    def scores_with(key_piece):
        count = key_piece.shape[1]
        keys = key_piece.reshape(seq_count, count, H, HD)
        raw = (
            jnp.einsum("sqhd,skhd->shqk", query_low, keys, preferred_element_type=jnp.float32)
            * 0.125
        )
        key_index = jnp.arange(count, dtype=jnp.int32)
        seen = (key_index[None, None, :] <= query_index[None, :, None]) & (
            key_index[None, None, :] >= first_seen[:, :, None]
        )
        return (raw, seen[:, None])

    start_top = jnp.full((seq_count, H, span_len), NEG, jnp.float32)
    raw, seen = scores_with(lax.all_gather(key_flat, "fsdp", axis=1, tiled=True))
    masked = jnp.where(seen, raw, NEG)
    new_top = jnp.maximum(start_top, jnp.max(masked, axis=-1))
    weights = jnp.where(seen, jnp.exp(masked - new_top[..., None]), 0.0)
    total = jnp.sum(weights, axis=-1)
    log_total = new_top + jnp.log(total)
    pieces = (
        lax.all_gather(key_flat, "fsdp", axis=1, tiled=True),
        lax.all_gather(value_flat, "fsdp", axis=1, tiled=True),
    )
    raw, seen = scores_with(pieces[0])
    count = pieces[1].shape[1]
    values = pieces[1].reshape(seq_count, count, H, HD)
    probs = jnp.where(seen, jnp.exp(raw - log_total[..., None]), 0.0)
    probs_low = probs.astype(jnp.bfloat16)
    residue = (probs - probs_low.astype(jnp.float32)).astype(jnp.bfloat16)
    mixed_sum = jnp.einsum("shqk,skhd->sqhd", probs_low, values, preferred_element_type=jnp.float32)
    residue_sum = jnp.einsum("shqk,skhd->sqhd", residue, values, preferred_element_type=jnp.float32)
    attended = mixed_sum.reshape(row_count, width).astype(jnp.bfloat16)
    hidden = jax.nn.gelu(up_full, approximate=False).astype(jnp.bfloat16)
    pieces = (
        lax.all_gather(w_out, "fsdp", axis=0, tiled=True),
        lax.all_gather(w_down, "fsdp", axis=0, tiled=True),
    )
    columns = jnp.einsum("rk,ck->rc", attended, pieces[0], preferred_element_type=jnp.float32)
    columns = columns + jnp.einsum(
        "rk,ck->rc", hidden, pieces[1], preferred_element_type=jnp.float32
    )
    output = (
        (source + columns + bias_out + bias_down).astype(jnp.bfloat16).reshape(layer_input.shape)
    )
    grad_out = cotangent.reshape(row_count, width)
    pieces = (
        lax.all_gather(w_out, "fsdp", axis=0, tiled=True),
        lax.all_gather(w_down, "fsdp", axis=0, tiled=True),
    )
    count = pieces[0].shape[0]
    grad_attended = jnp.dot(grad_out, pieces[0], preferred_element_type=jnp.float32)
    grad_hidden = jnp.dot(grad_out, pieces[1], preferred_element_type=jnp.float32)
    grad_mixed = grad_attended.astype(jnp.bfloat16)
    gelu_value, pull_gelu = jax.vjp(lambda v: jax.nn.gelu(v, approximate=False), up_full)
    grad_up = pull_gelu(grad_hidden)[0].astype(jnp.bfloat16)
    grad_heads = grad_mixed.reshape(seq_count, span_len, H, HD)
    carried = jnp.sum(grad_heads.astype(jnp.float32) * (mixed_sum + residue_sum), axis=-1)
    carried_rows = jnp.transpose(carried, (0, 2, 1))
    pieces = (
        lax.all_gather(key_flat, "fsdp", axis=1, tiled=True),
        lax.all_gather(value_flat, "fsdp", axis=1, tiled=True),
    )
    raw, seen = scores_with(pieces[0])
    count = pieces[0].shape[1]
    keys = pieces[0].reshape(seq_count, count, H, HD)
    values = pieces[1].reshape(seq_count, count, H, HD)
    probs = jnp.where(seen, jnp.exp(raw - log_total[..., None]), 0.0)
    probs_low = probs.astype(jnp.bfloat16)
    grad_probs = jnp.einsum(
        "sqhd,skhd->shqk", grad_heads, values, preferred_element_type=jnp.float32
    )
    grad_scores = (probs * (grad_probs - carried_rows[..., None])).astype(jnp.bfloat16)
    grad_query = jnp.einsum(
        "shqk,skhd->sqhd", grad_scores, keys, preferred_element_type=jnp.float32
    )
    key_part = jnp.einsum(
        "shqk,sqhd->skhd", grad_scores, query_low, preferred_element_type=jnp.float32
    )
    value_part = jnp.einsum(
        "shqk,sqhd->skhd", probs_low, grad_heads, preferred_element_type=jnp.float32
    )
    both = jnp.concatenate(
        [key_part.reshape(seq_count, count, width), value_part.reshape(seq_count, count, width)],
        axis=2,
    )
    key_terms = both
    grad_query, key_terms = (grad_query, key_terms)
    grad_query = grad_query * 0.125
    key_owned = lax.psum_scatter(key_terms, "fsdp", scatter_dimension=1, tiled=True)
    grad_key = key_owned[..., :width].reshape(seq_count, span_len, H, HD) * 0.125
    grad_value = key_owned[..., width:].reshape(seq_count, span_len, H, HD)
    grad_qkv = pull_turn((grad_query, grad_key, grad_value))[0].astype(jnp.bfloat16)
    pieces = (
        lax.all_gather(w_qkv, "fsdp", axis=0, tiled=True),
        lax.all_gather(w_up, "fsdp", axis=0, tiled=True),
    )
    columns_one = jnp.einsum("rk,ck->rc", grad_qkv, pieces[0], preferred_element_type=jnp.float32)
    columns_two = jnp.einsum("rk,ck->rc", grad_up, pieces[1], preferred_element_type=jnp.float32)
    grad_source_one, grad_gain_one, grad_shift_one = pull_one(columns_one)
    grad_source_two, grad_gain_two, grad_shift_two = pull_two(columns_two)
    grad_out_float = grad_out.astype(jnp.float32)
    grad_input = (
        (grad_out_float + grad_source_one + grad_source_two)
        .astype(jnp.bfloat16)
        .reshape(layer_input.shape)
    )
    grad_out_total = jnp.sum(grad_out_float, axis=0)
    local_vectors = (
        grad_gain_one,
        grad_shift_one,
        grad_gain_two,
        grad_shift_two,
        jnp.sum(grad_qkv.astype(jnp.float32), axis=0),
        grad_out_total,
        jnp.sum(grad_up.astype(jnp.float32), axis=0),
    )
    summed = lax.psum(
        (
            local_vectors[0],
            local_vectors[1],
            local_vectors[2],
            local_vectors[3],
            local_vectors[4],
            local_vectors[5],
            local_vectors[6],
        ),
        ("rep", "fsdp"),
    )
    owned_vectors = [
        lax.dynamic_slice_in_dim(
            v, shard_index * (v.shape[0] // shard_count), v.shape[0] // shard_count
        )
        for v in summed
    ]
    owned = lax.psum_scatter(
        jnp.concatenate(
            [
                jnp.einsum("rc,rk->ck", input_one, grad_qkv, preferred_element_type=jnp.float32),
                jnp.einsum("rc,rk->ck", grad_out, attended, preferred_element_type=jnp.float32),
                jnp.einsum("rc,rk->ck", input_two, grad_up, preferred_element_type=jnp.float32),
                jnp.einsum("rc,rk->ck", grad_out, hidden, preferred_element_type=jnp.float32),
            ],
            axis=1,
        ),
        "fsdp",
        scatter_dimension=0,
        tiled=True,
    )
    owned = lax.psum(owned, "rep")
    edge_two = qkv_cols + width
    edge_three = edge_two + hidden_cols
    grad_w_qkv = owned[:, :qkv_cols]
    grad_w_out = owned[:, qkv_cols:edge_two]
    grad_w_up = owned[:, edge_two:edge_three]
    grad_w_down = owned[:, edge_three:]
    return (
        output,
        grad_input,
        grad_w_qkv,
        grad_w_out,
        grad_w_up,
        grad_w_down,
        owned_vectors[0],
        owned_vectors[1],
        owned_vectors[2],
        owned_vectors[3],
        owned_vectors[4],
        owned_vectors[5],
        owned_vectors[6],
        owned_vectors[5],
    )


def solution(mesh):
    return jax.shard_map(
        on_device,
        mesh=mesh,
        in_specs=(
            P("rep", "fsdp", None),
            P("rep", "fsdp"),
            P("rep", "fsdp", None),
            P("fsdp", None),
            P("fsdp", None),
            P("fsdp", None),
            P("fsdp", None),
            P("fsdp"),
            P("fsdp"),
            P("fsdp"),
            P("fsdp"),
            P("fsdp"),
            P("fsdp"),
            P("fsdp"),
            P("fsdp"),
        ),
        out_specs=(
            P("rep", "fsdp", None),
            P("rep", "fsdp", None),
            P("fsdp", None),
            P("fsdp", None),
            P("fsdp", None),
            P("fsdp", None),
            P("fsdp"),
            P("fsdp"),
            P("fsdp"),
            P("fsdp"),
            P("fsdp"),
            P("fsdp"),
            P("fsdp"),
            P("fsdp"),
        ),
        check_vma=False,
    )
```

profile of v0, /device:TPU:0, one launch (start us, length us, event | category | flops | bytes accessed | tf_op | source)
XLA Modules:
  0.0 780.7 jit_solution(14124956346842506521)
XLA Ops:
  21.0 26.5 %all-reduce.19 = (bf16[768]{0:T(1024)(128)(2,1)S(1)}, bf16[768]{0:T(1024)(128)(2,1)S(1)}, bf16[768]{0:T(1024)(128)(2,1)}, bf16[768]{0:T(1024)(128)(2,1)}, bf16[7...) all-reduce(bf16[768]{0:T(1024)(128)(2,1)S(1)} %dynamic-update-slice, ...), channel_id=1, replica_groups=mesh['rep'=4,'fsdp'=8] {'fsdp'}, use_global_device_ids=true, to_apply=%add.15 | all-reduce | flops 6912 | bytes 27648
  49.2 6.1 convolution_add_fusion
  55.4 6.2 copy.46
  61.5 6.3 reshape.249
  84.6 37.4 %all-gather.12.cloned.1.call-done = bf16[4,1024,768]{1,2,0:T(8,128)(2,1)} async-done(((bf16[4,128,768]{1,2,0:T(8,128)(2,1)}), bf16[4,1024,768]{1,2,0:T(8,128)(2,1)}) %all-gather.12.cloned.1.call-update) | async-done | bytes 6291472 | tf_op jit(solution)/shard_map/all_gather | solution.py:124
  121.9 12.9 %select_reduce_fusion.1 = (f32[4,12,128]{2,1,0:T(8,128)S(1)}, f32[4,12,128,1024]{3,2,1,0:T(8,128)}) fusion(pred[4,128,1024]{2,1,0:T(8,128)(4,1)S(1)} %fusion.13, bf16[4,1024,12,64]{1,3,2,0:T(8,128)(2,1)} %bitcast.164, bf16[4,128,12,48]{1,3,2,0:T(8,128)(2,1)S(1)} %slice.110, bf16[4,128,12,16]{1,3,2,0:T(8,128)(2,1)S(1)} %get-tuple-element.61), kind=kOutput, calls=%fused_computation.6 | convolution fusion | flops 825747456 | bytes 32792576 | tf_op jit(solution)/shard_map/sqhd,skhd->shqk/dot_general | solution.py:107
  134.9 12.2 %select_reduce_fusion = f32[4,12,128]{2,1,0:T(8,128)S(1)} fusion(f32[4,12,128,1024]{3,2,1,0:T(8,128)} %get-tuple-element.76, f32[4,12,128]{2,1,0:T(8,128)S(1)} %broadcast_maximum_fusion, pred[4,128,1024]{2,1,0:T(8,128)(4,1)S(1)} %fusion.13), kind=kLoop, calls=%fused_computation.5 | loop fusion | flops 31451136 | bytes 25739264 | tf_op jit(solution)/shard_map/reduce_sum | solution.py:121
  147.1 23.9 %all-gather.10.cloned.1.call-done = bf16[4,1024,768]{1,2,0:T(8,128)(2,1)} async-done(((bf16[4,128,768]{1,2,0:T(8,128)(2,1)}), bf16[4,1024,768]{1,2,0:T(8,128)(2,1)}) %all-gather.10.cloned.1.call-update) | async-done | bytes 6291472 | tf_op jit(solution)/shard_map/all_gather | solution.py:125
  170.9 14.2 %fusion.58 = f32[4,12,64,128]{3,2,1,0:T(8,128)} fusion(bf16[4,1024,12,64]{1,3,2,0:T(8,128)(2,1)} %bitcast.190, f32[4,12,128,1024]{3,2,1,0:T(8,128)} %get-tuple-element.76, f32[4,12,128]{2,1,0:T(8,128)S(1)} %log_add_fusion, pred[4,128,1024]{2,1,0:T(8,128)(4,1)S(1)} %fusion.13), kind=kOutput, calls=%fused_computation.110 | convolution fusion | flops 830472192 | bytes 33579008 | tf_op jit(solution)/shard_map/shqk,skhd->sqhd/dot_general | solution.py:133
  185.2 15.0 %fusion.16 = f32[4,128,12]{1,2,0:T(8,128)S(1)} fusion(f32[4,12,64,128]{3,2,1,0:T(8,128)} %fusion.58, bf16[4,1024,12,64]{1,3,2,0:T(8,128)(2,1)} %bitcast.191, f32[4,12,128,1024]{3,2,1,0:T(8,128)} %get-tuple-element.76, f32[4,12,128]{2,1,0:T(8,128)S(1)} %log_add_fusion, pred[4,128,1024]{2,1,0:T(8,128)(4,1)S(1)} %fusion.13, bf16[4,128,12,64]{1,0,3,2:T(4,128)(2,1)} %reshape.254), kind=kOutput, calls=%fused_computation.48 | convolution fusion | flops 850913280 | bytes 34390016 | tf_op jit(solution)/shard_map/shqk,skhd->sqhd/dot_general | solution.py:134
  200.2 20.5 %multiply_convert_fusion = bf16[4,12,128,1024]{3,2,1,0:T(8,128)(2,1)} fusion(f32[4,12,128,1024]{3,2,1,0:T(8,128)} %get-tuple-element.76, f32[4,12,128]{2,1,0:T(8,128)S(1)} %bitcast.194, f32[4,12,128]{2,1,0:T(8,128)S(1)} %log_add_fusion, pred[4,128,1024]{2,1,0:T(8,128)(4,1)S(1)} %fusion.13, bf16[4,1024,12,64]{1,3,2,0:T(8,128)(2,1)} %bitcast.192, ...), kind=kOutput, calls=%fused_computation.2 | convolution fusion | flops 843055104 | bytes 45400064 | tf_op jit(solution)/shard_map/sqhd,skhd->shqk/dot_general | solution.py:172
  220.6 11.1 %fusion.50 = f32[4,12,64,1024]{3,2,1,0:T(8,128)} fusion(bf16[4,12,128,1024]{3,2,1,0:T(8,128)(2,1)} %multiply_convert_fusion, bf16[4,128,12,48]{1,3,2,0:T(8,128)(2,1)S(1)} %slice.110, bf16[4,128,12,16]{1,3,2,0:T(8,128)(2,1)S(1)} %get-tuple-element.61), kind=kOutput, calls=%fused_computation.98 | convolution fusion | flops 806879232 | bytes 25952256 | tf_op jit(solution)/shard_map/shqk,sqhd->skhd/dot_general | solution.py:179
  231.8 14.8 %fusion.47 = f32[4,12,64,1024]{3,2,1,0:T(8,128)} fusion(bf16[4,128,12,64]{1,0,3,2:T(4,128)(2,1)S(1)} %copy-done.12, f32[4,12,128,1024]{3,2,1,0:T(8,128)} %get-tuple-element.76, f32[4,12,128]{2,1,0:T(8,128)S(1)} %log_add_fusion, pred[4,128,1024]{2,1,0:T(8,128)(4,1)S(1)} %fusion.13), kind=kOutput, calls=%fused_computation.94 | convolution fusion | flops 830472192 | bytes 39084032 | tf_op jit(solution)/shard_map/shqk,sqhd->skhd/dot_general | solution.py:182
  246.5 18.8 %pad_maximum_fusion.1 = f32[4,1024,1536]{1,2,0:T(8,128)} fusion(f32[4,1024,768]{1,2,0:T(8,128)} %bitcast.163, f32[4,1024,768]{1,2,0:T(8,128)} %bitcast.162), kind=kLoop, calls=%fused_computation.1 | loop fusion | flops 6291456 | bytes 50331648 | tf_op jit(solution)/shard_map/concatenate | solution.py:185
  266.0 9.4 %all-gather = bf16[8,1,384]{2,1,0:T(2,128)(2,1)S(1)} all-gather(bf16[1,1,384]{2,1,0:T(2,128)(2,1)S(1)} %reshape.280), channel_id=1, replica_groups=mesh['rep'=4,'fsdp'=8] {'fsdp'}, dimensions={0}, use_global_device_ids=true | all-gather | bytes 6912 | tf_op jit(solution)/shard_map/all_gather | solution.py:64
  276.7 8.9 %fusion.83 = f32[512,3072]{1,0:T(8,128)} fusion(bf16[512,768]{1,0:T(8,128)(2,1)S(1)} %get-tuple-element.54, bf16[768,3072]{1,0:T(8,128)(2,1)} %all-gather.16.cloned.1.call-done), kind=kOutput, calls=%fused_computation.154 | convolution fusion | flops 2415919104 | bytes 11796480 | tf_op jit(solution)/shard_map/dot_general | solution.py:81
  285.6 19.4 %convert_reduce_fusion = (f32[3072]{0:T(1024)S(1)}, bf16[512,3072]{1,0:T(8,128)(2,1)S(1)}, f32[512,3072]{1,0:T(8,128)S(1)}) fusion(f32[512,3072]{1,0:T(8,128)} %fusion.83, f32[3072]{0:T(1024)S(1)} %bitcast.188, bf16[512,768]{1,0:T(8,128)(2,1)S(1)} %bitcast.170, bf16[768,3072]{1,0:T(8,128)(2,1)} %all-gather.18.cloned.1.call-done), kind=kOutput, calls=%fused_computation.12 | convolution fusion | flops 2533880832 | bytes 21258240 | tf_op jit(solution)/shard_map/dot_general | solution.py:155
  308.2 7.8 convolution_bitcast_fusion
  321.2 11.3 %multiply_bitcast_fusion = f32[4,128,12,64]{1,3,2,0:T(8,128)S(1)} fusion(bf16[4,1024,12,64]{1,3,2,0:T(8,128)(2,1)} %bitcast.165, bf16[4,12,128,1024]{3,2,1,0:T(8,128)(2,1)} %multiply_convert_fusion), kind=kOutput, calls=%fused_computation.82 | convolution fusion | flops 805699584 | bytes 20447232 | tf_op jit(solution)/shard_map/shqk,skhd->sqhd/dot_general | solution.py:176
  340.6 82.4 %reduce-scatter.3.cloned.1.call-done = f32[4,128,1536]{1,2,0:T(8,128)} async-done(((f32[4,1024,1536]{1,2,0:T(8,128)}), f32[4,128,1536]{1,2,0:T(8,128)}) %reduce-scatter.3.cloned.1.call-update) | async-done | bytes 3145744 | tf_op jit(solution)/shard_map/reduce_scatter | solution.py:192
  436.1 19.4 %pad_maximum_fusion = f32[768,9216]{1,0:T(8,128)} fusion(f32[768,3072]{1,0:T(8,128)} %convolution_bitcast_fusion, f32[768,3072]{1,0:T(8,128)} %fusion.86, f32[768,768]{1,0:T(8,128)S(1)} %copy.57, f32[768,2304]{1,0:T(8,128)} %fusion.9), kind=kLoop, calls=%fused_computation | loop fusion | flops 21233664 | bytes 56623104 | tf_op jit(solution)/shard_map/concatenate | solution.py:239
  456.4 172.6 %reduce-scatter.5.cloned.1.call-done = f32[96,9216]{1,0:T(8,128)} async-done(((f32[768,9216]{1,0:T(8,128)}), f32[96,9216]{1,0:T(8,128)}) %reduce-scatter.5.cloned.1.call-update) | async-done | bytes 3538960 | tf_op jit(solution)/shard_map/reduce_scatter | solution.py:238
  650.8 44.4 %all-reduce.18 = (f32[768]{0:T(1024)S(1)}, f32[768]{0:T(1024)S(1)}, f32[768]{0:T(1024)S(1)}, f32[768]{0:T(1024)S(1)}, f32[2304]{0:T(1024)S(1)}, /*index=5*/f32[768]{0:T(1024)S(1)}, f32[3072]{0:T(1024)S(1)}) all-reduce(f32[768]{0:T(1024)S(1)} %get-tuple-element.23, ...), channel_id=1, replica_groups=mesh['rep'=4,'fsdp'=8] {'rep','fsdp'}, use_global_device_ids=true, to_apply=%region_13.14 | all-reduce | flops 9216 | bytes 73728 | tf_op jit(solution)/shard_map/psum | solution.py:220
  701.9 64.2 %all-reduce.22.cloned.1.call-done = f32[96,9216]{1,0:T(8,128)} async-done(((f32[96,9216]{1,0:T(8,128)}), f32[96,9216]{1,0:T(8,128)}) %all-reduce.22.cloned.1.call-update) | async-done | bytes 3538960 | tf_op jit(solution)/shard_map/psum | solution.py:252
  (184 shorter events, 98.8 us)
Async XLA Ops:
  7.2 42.0 %all-gather.8.cloned.1.call-start = ((), (), s32[]{:S(2)}) async-start(), calls=%async_computation.2 | async-start | bytes 3981312 | tf_op jit(solution)/shard_map/all_gather | solution.py:76
  7.9 69.8 %all-gather.14.cloned.1.call-start = ((), (), s32[]{:S(2)}) async-start(), calls=%async_computation.5 | async-start | bytes 1327104 | tf_op jit(solution)/shard_map/all_gather | solution.py:138
  8.7 113.3 %all-gather.12.cloned.1.call-start = ((), (), s32[]{:S(2)}) async-start(), calls=%async_computation.4 | async-start | bytes 7077888 | tf_op jit(solution)/shard_map/all_gather | solution.py:124
  10.0 45.3 %copy-start.23 = (f32[512]{0:T(512)}, f32[512]{0:T(512)S(1)}, u32[]{:S(2)}) copy-start(f32[512]{0:T(512)S(1)} %get-tuple-element.73) | copy-start | bytes 6148
  11.6 263.9 %copy-start.27 = (f32[4,128]{1,0:T(4,128)}, f32[4,128]{1,0:T(4,128)S(1)}, u32[]{:S(2)}) copy-start(f32[4,128]{1,0:T(4,128)S(1)} %fusion.28) | copy-start | bytes 6148
  12.5 58.2 %copy-start.15 = (f32[4,128,16]{1,2,0:T(8,128)}, f32[4,128,16]{1,2,0:T(8,128)S(1)}, u32[]{:S(2)}) copy-start(f32[4,128,16]{1,2,0:T(8,128)S(1)} %get-tuple-element.67) | copy-start | bytes 98308
  12.5 58.2 %copy-start.17 = (f32[4,128,16]{1,2,0:T(8,128)}, f32[4,128,16]{1,2,0:T(8,128)S(1)}, u32[]{:S(2)}) copy-start(f32[4,128,16]{1,2,0:T(8,128)S(1)} %get-tuple-element.68) | copy-start | bytes 98308
  47.5 228.0 %copy-start.19 = (f32[768]{0:T(1024)}, f32[768]{0:T(1024)S(1)}, u32[]{:S(2)}) copy-start(f32[768]{0:T(1024)S(1)} %convert_element_type.126) | copy-start | bytes 9220
  47.5 7.9 %copy-start.21 = (f32[768]{0:T(1024)}, f32[768]{0:T(1024)S(1)}, u32[]{:S(2)}) copy-start(f32[768]{0:T(1024)S(1)} %convert_element_type.137) | copy-start | bytes 9220
  47.6 7.8 copy-start.25
  72.8 98.1 %all-gather.10.cloned.1.call-start = ((), (), s32[]{:S(2)}) async-start(), calls=%async_computation.3 | async-start | bytes 7077888 | tf_op jit(solution)/shard_map/all_gather | solution.py:125
  75.6 201.1 %all-gather.16.cloned.1.call-start = ((), (), s32[]{:S(2)}) async-start(), calls=%async_computation.6 | async-start | bytes 5308416 | tf_op jit(solution)/shard_map/all_gather | solution.py:77
  76.2 209.3 %all-gather.18.cloned.1.call-start = ((), (), s32[]{:S(2)}) async-start(), calls=%async_computation.7 | async-start | bytes 5308416 | tf_op jit(solution)/shard_map/all_gather | solution.py:139
  76.8 346.2 %reduce-scatter.3.cloned.1.call-start = ((), (), s32[]{:S(2)}) async-start(), calls=%async_computation.8 | async-start | bytes 28311552 | tf_op jit(solution)/shard_map/reduce_scatter | solution.py:192
  220.6 11.1 %copy-start.12 = (bf16[4,128,12,64]{1,0,3,2:T(4,128)(2,1)S(1)}, bf16[4,128,12,64]{1,0,3,2:T(4,128)(2,1)}, u32[]{:S(2)}) copy-start(bf16[4,128,12,64]{1,0,3,2:T(4,128)(2,1)} %reshape.254) | copy-start | bytes 2359300
  265.3 10.1 %copy-start = (bf16[4,128,768]{2,1,0:T(8,128)(2,1)S(1)}, bf16[4,128,768]{2,1,0:T(8,128)(2,1)}, u32[]{:S(2)}) copy-start(bf16[4,128,768]{2,1,0:T(8,128)(2,1)} %param.15) | copy-start | bytes 2359300
  265.3 363.6 %reduce-scatter.5.cloned.1.call-start = ((), (), s32[]{:S(2)}) async-start(), calls=%async_computation.9 | async-start | bytes 31850496 | tf_op jit(solution)/shard_map/reduce_scatter | solution.py:238
  285.6 19.4 %copy-start.2 = (f32[512,3072]{1,0:T(8,128)S(1)}, f32[512,3072]{1,0:T(8,128)}, u32[]{:S(2)}) copy-start(f32[512,3072]{1,0:T(8,128)} %fusion.83) | copy-start | bytes 18874372
  305.0 11.0 %copy-start.8 = (bf16[512,3072]{1,0:T(8,128)(2,1)}, bf16[512,3072]{1,0:T(8,128)(2,1)S(1)}, u32[]{:S(2)}) copy-start(bf16[512,3072]{1,0:T(8,128)(2,1)S(1)} %get-tuple-element.39) | copy-start | bytes 9437188
  338.5 86.7 %copy-start.18 = (f32[4,128,16]{1,2,0:T(8,128)S(1)}, f32[4,128,16]{1,2,0:T(8,128)}, u32[]{:S(2)}) copy-start(f32[4,128,16]{1,2,0:T(8,128)} %copy-done.17) | copy-start | bytes 98308
  340.6 85.1 %copy-start.16 = (f32[4,128,16]{1,2,0:T(8,128)S(1)}, f32[4,128,16]{1,2,0:T(8,128)}, u32[]{:S(2)}) copy-start(f32[4,128,16]{1,2,0:T(8,128)} %copy-done.15) | copy-start | bytes 98308
  455.5 310.6 %all-reduce.22.cloned.1.call-start = ((), (), s32[]{:S(2)}) async-start(), calls=%async_computation.10 | async-start | bytes 7077888 | tf_op jit(solution)/shard_map/psum | solution.py:252
  642.9 6.5 copy-start.26
  695.3 78.0 %copy-start.33 = (f32[96]{0:T(128)}, f32[96]{0:T(128)S(1)}, u32[]{:S(2)}) copy-start(f32[96]{0:T(128)S(1)} %dynamic_slice.26) | copy-start | bytes 1156
  (20 other events, 58.3 us)
Sparse Core Ops, SparseCore 0:
  9.9 36.8 all-gather.7
  48.7 24.0 all-gather.13
  75.2 46.6 all-gather.11
  124.2 46.6 all-gather.9
  172.7 38.9 all-gather.15
  213.4 38.8 all-gather.17
  265.5 157.4 reduce-scatter.2
  455.7 173.2 reduce-scatter.4
  631.3 134.7 all-reduce.21
where the time goes:
time: 787 us; the launch traced here: 781 us
  waiting for transfers between devices  383 us (49%)
  matrix products  176 us (22%)
  blocking collectives  80.3 us (10%)
  other arithmetic  72.3 us (9%)
  local copies, waits for them, and re-layouts  51.7 us (7%)
  between operations  16.3 us (2%)
    reduce_scatter x1, waiting for transfers between devices, on_device(): lax.psum_scatter(jnp.concatenate([jnp.einsum('rc,rk->ck', input_one, grad...  173 us
    reduce_scatter x1, waiting for transfers between devices, on_device(): lax.psum_scatter(key_terms, 'fsdp', scatter_dimension=1, tiled=True)  82.4 us
    psum x1, waiting for transfers between devices, on_device(): owned = lax.psum(owned, 'rep')  64.2 us
    psum x1, blocking collectives, on_device(): lax.psum((local_vectors[0], local_vectors[1], local_vectors[2], local_vec...  44.4 us
    all_gather x1, waiting for transfers between devices, on_device(): lax.all_gather(key_flat, 'fsdp', axis=1, tiled=True)  37.4 us
    unnamed x1, blocking collectives  26.5 us
    all_gather x1, waiting for transfers between devices, on_device(): lax.all_gather(value_flat, 'fsdp', axis=1, tiled=True)  23.9 us
    dot_general x1, matrix products, on_device(): jnp.einsum('sqhd,skhd->shqk', grad_heads, values, preferred_element_type=...  20.5 us
  transfers between devices with their start and end apart: 9, of which 5 were waited for; matrix products, arithmetic and copies ran while one was open for 33% of the time, Pallas kernels for 0%

commit v1 on v0

--- a/solution.py
+++ b/solution.py
@@ -249,7 +249,9 @@
         scatter_dimension=0,
         tiled=True,
     )
-    owned = lax.psum(owned, "rep")
+    owned = owned
+    for hop in (1, 2):
+        owned = owned + lax.ppermute(owned, "rep", [(dev, dev ^ hop) for dev in range(4)])
     edge_two = qkv_cols + width
     edge_three = edge_two + hidden_cols
     grad_w_qkv = owned[:, :qkv_cols]

time: 787 us -> 917 us (1.17)
  blocking collectives: 80.3 us -> 194 us
  waiting for transfers between devices: 383 us -> 397 us
    psum x1, blocking collectives: 44.4 us -> 158 us  [on_device(): lax.psum((local_vectors[0], local_vectors[1], local_vectors[2], local_vec...]
    ppermute x0 -> x2, waiting for transfers between devices: none -> 76.9 us  [on_device(): lax.ppermute(owned, 'rep', [(dev, dev ^ hop) for dev in range(4)])]
    psum x1 -> x0, waiting for transfers between devices: 64.2 us -> none  [on_device(): owned = lax.psum(owned, 'rep')]
  transfers between devices with their start and end apart: 9 -> 10, of which waited for: 5 -> 5; matrix products, arithmetic and copies ran while one was open for 33% -> 27% of each run, Pallas kernels for 0% -> 0%
where the time goes in v1:
time: 917 us; the launch traced here: 910 us
  waiting for transfers between devices  397 us (43%)
  blocking collectives  194 us (21%)
  matrix products  170 us (19%)
  other arithmetic  81.2 us (9%)
  local copies, waits for them, and re-layouts  47.7 us (5%)
  between operations  16.6 us (2%)
    reduce_scatter x1, waiting for transfers between devices, on_device(): lax.psum_scatter(jnp.concatenate([jnp.einsum('rc,rk->ck', input_one, grad...  173 us
    psum x1, blocking collectives, on_device(): lax.psum((local_vectors[0], local_vectors[1], local_vectors[2], local_vec...  158 us
    reduce_scatter x1, waiting for transfers between devices, on_device(): lax.psum_scatter(key_terms, 'fsdp', scatter_dimension=1, tiled=True)  82.4 us
    ppermute x2, waiting for transfers between devices, on_device(): lax.ppermute(owned, 'rep', [(dev, dev ^ hop) for dev in range(4)])  76.9 us
    all_gather x1, waiting for transfers between devices, on_device(): lax.all_gather(key_flat, 'fsdp', axis=1, tiled=True)  37.4 us
    unnamed x1, blocking collectives  26.5 us
    all_gather x1, waiting for transfers between devices, on_device(): lax.all_gather(value_flat, 'fsdp', axis=1, tiled=True)  23.9 us
    dot_general x1, matrix products, on_device(): jnp.einsum('sqhd,skhd->shqk', grad_heads, values, preferred_element_type=...  20.5 us
  transfers between devices with their start and end apart: 10, of which 5 were waited for; matrix products, arithmetic and copies ran while one was open for 27% of the time, Pallas kernels for 0%

profile of v1, /device:TPU:0, one launch (start us, length us, event | category | flops | bytes accessed | tf_op | source)
XLA Modules:
  0.0 910.2 jit_solution(17819985086039123683)
XLA Ops:
  21.0 26.5 %all-reduce.19 = (bf16[768]{0:T(1024)(128)(2,1)S(1)}, bf16[768]{0:T(1024)(128)(2,1)S(1)}, bf16[768]{0:T(1024)(128)(2,1)}, bf16[768]{0:T(1024)(128)(2,1)}, bf16[7...) all-reduce(bf16[768]{0:T(1024)(128)(2,1)S(1)} %dynamic-update-slice, ...), channel_id=1, replica_groups=mesh['rep'=4,'fsdp'=8] {'fsdp'}, use_global_device_ids=true, to_apply=%add.15 | all-reduce | flops 6912 | bytes 27648
  49.2 6.2 convolution_add_fusion
  55.4 6.2 copy.46
  61.5 6.4 reshape.249
  84.5 37.4 %all-gather.12.cloned.1.call-done = bf16[4,1024,768]{1,2,0:T(8,128)(2,1)} async-done(((bf16[4,128,768]{1,2,0:T(8,128)(2,1)}), bf16[4,1024,768]{1,2,0:T(8,128)(2,1)}) %all-gather.12.cloned.1.call-update) | async-done | bytes 6291472 | tf_op jit(solution)/shard_map/all_gather | solution.py:124
  121.9 12.9 %select_reduce_fusion.1 = (f32[4,12,128]{2,1,0:T(8,128)S(1)}, f32[4,12,128,1024]{3,2,1,0:T(8,128)}) fusion(pred[4,128,1024]{2,1,0:T(8,128)(4,1)S(1)} %fusion.13, bf16[4,1024,12,64]{1,3,2,0:T(8,128)(2,1)} %bitcast.164, bf16[4,128,12,48]{1,3,2,0:T(8,128)(2,1)S(1)} %slice.110, bf16[4,128,12,16]{1,3,2,0:T(8,128)(2,1)S(1)} %get-tuple-element.61), kind=kOutput, calls=%fused_computation.6 | convolution fusion | flops 825747456 | bytes 32792576 | tf_op jit(solution)/shard_map/sqhd,skhd->shqk/dot_general | solution.py:107
  134.9 12.2 %select_reduce_fusion = f32[4,12,128]{2,1,0:T(8,128)S(1)} fusion(f32[4,12,128,1024]{3,2,1,0:T(8,128)} %get-tuple-element.76, f32[4,12,128]{2,1,0:T(8,128)S(1)} %broadcast_maximum_fusion, pred[4,128,1024]{2,1,0:T(8,128)(4,1)S(1)} %fusion.13), kind=kLoop, calls=%fused_computation.5 | loop fusion | flops 31451136 | bytes 25739264 | tf_op jit(solution)/shard_map/reduce_sum | solution.py:121
  147.1 23.9 %all-gather.10.cloned.1.call-done = bf16[4,1024,768]{1,2,0:T(8,128)(2,1)} async-done(((bf16[4,128,768]{1,2,0:T(8,128)(2,1)}), bf16[4,1024,768]{1,2,0:T(8,128)(2,1)}) %all-gather.10.cloned.1.call-update) | async-done | bytes 6291472 | tf_op jit(solution)/shard_map/all_gather | solution.py:125
  170.9 14.2 %fusion.58 = f32[4,12,64,128]{3,2,1,0:T(8,128)} fusion(bf16[4,1024,12,64]{1,3,2,0:T(8,128)(2,1)} %bitcast.192, f32[4,12,128,1024]{3,2,1,0:T(8,128)} %get-tuple-element.76, f32[4,12,128]{2,1,0:T(8,128)S(1)} %log_add_fusion, pred[4,128,1024]{2,1,0:T(8,128)(4,1)S(1)} %fusion.13), kind=kOutput, calls=%fused_computation.110 | convolution fusion | flops 830472192 | bytes 33579008 | tf_op jit(solution)/shard_map/shqk,skhd->sqhd/dot_general | solution.py:133
  185.1 15.0 %fusion.16 = f32[4,128,12]{1,2,0:T(8,128)S(1)} fusion(f32[4,12,64,128]{3,2,1,0:T(8,128)} %fusion.58, bf16[4,1024,12,64]{1,3,2,0:T(8,128)(2,1)} %bitcast.193, f32[4,12,128,1024]{3,2,1,0:T(8,128)} %get-tuple-element.76, f32[4,12,128]{2,1,0:T(8,128)S(1)} %log_add_fusion, pred[4,128,1024]{2,1,0:T(8,128)(4,1)S(1)} %fusion.13, bf16[4,128,12,64]{1,0,3,2:T(4,128)(2,1)} %reshape.254), kind=kOutput, calls=%fused_computation.48 | convolution fusion | flops 850913280 | bytes 34390016 | tf_op jit(solution)/shard_map/shqk,skhd->sqhd/dot_general | solution.py:134
  200.2 20.5 %multiply_convert_fusion = bf16[4,12,128,1024]{3,2,1,0:T(8,128)(2,1)} fusion(f32[4,12,128,1024]{3,2,1,0:T(8,128)} %get-tuple-element.76, f32[4,12,128]{2,1,0:T(8,128)S(1)} %bitcast.198, f32[4,12,128]{2,1,0:T(8,128)S(1)} %log_add_fusion, pred[4,128,1024]{2,1,0:T(8,128)(4,1)S(1)} %fusion.13, bf16[4,1024,12,64]{1,3,2,0:T(8,128)(2,1)} %bitcast.194, ...), kind=kOutput, calls=%fused_computation.2 | convolution fusion | flops 843055104 | bytes 45400064 | tf_op jit(solution)/shard_map/sqhd,skhd->shqk/dot_general | solution.py:172
  220.6 11.1 %fusion.50 = f32[4,12,64,1024]{3,2,1,0:T(8,128)} fusion(bf16[4,12,128,1024]{3,2,1,0:T(8,128)(2,1)} %multiply_convert_fusion, bf16[4,128,12,48]{1,3,2,0:T(8,128)(2,1)S(1)} %slice.110, bf16[4,128,12,16]{1,3,2,0:T(8,128)(2,1)S(1)} %get-tuple-element.61), kind=kOutput, calls=%fused_computation.98 | convolution fusion | flops 806879232 | bytes 25952256 | tf_op jit(solution)/shard_map/shqk,sqhd->skhd/dot_general | solution.py:179
  231.8 14.7 %fusion.47 = f32[4,12,64,1024]{3,2,1,0:T(8,128)} fusion(bf16[4,128,12,64]{1,0,3,2:T(4,128)(2,1)S(1)} %copy-done.13, f32[4,12,128,1024]{3,2,1,0:T(8,128)} %get-tuple-element.76, f32[4,12,128]{2,1,0:T(8,128)S(1)} %log_add_fusion, pred[4,128,1024]{2,1,0:T(8,128)(4,1)S(1)} %fusion.13), kind=kOutput, calls=%fused_computation.94 | convolution fusion | flops 830472192 | bytes 39084032 | tf_op jit(solution)/shard_map/shqk,sqhd->skhd/dot_general | solution.py:182
  246.5 18.7 %pad_maximum_fusion.1 = f32[4,1024,1536]{1,2,0:T(8,128)} fusion(f32[4,1024,768]{1,2,0:T(8,128)} %bitcast.163, f32[4,1024,768]{1,2,0:T(8,128)} %bitcast.162), kind=kLoop, calls=%fused_computation.1 | loop fusion | flops 6291456 | bytes 50331648 | tf_op jit(solution)/shard_map/concatenate | solution.py:185
  266.0 9.5 %all-gather = bf16[8,1,384]{2,1,0:T(2,128)(2,1)S(1)} all-gather(bf16[1,1,384]{2,1,0:T(2,128)(2,1)S(1)} %reshape.280), channel_id=1, replica_groups=mesh['rep'=4,'fsdp'=8] {'fsdp'}, dimensions={0}, use_global_device_ids=true | all-gather | bytes 6912 | tf_op jit(solution)/shard_map/all_gather | solution.py:64
  276.7 8.8 fusion.83
  285.6 19.4 %convert_reduce_fusion = (f32[3072]{0:T(1024)S(1)}, bf16[512,3072]{1,0:T(8,128)(2,1)S(1)}, f32[512,3072]{1,0:T(8,128)S(1)}) fusion(f32[512,3072]{1,0:T(8,128)} %fusion.83, f32[3072]{0:T(1024)S(1)} %bitcast.190, bf16[512,768]{1,0:T(8,128)(2,1)S(1)} %bitcast.170, bf16[768,3072]{1,0:T(8,128)(2,1)} %all-gather.18.cloned.1.call-done), kind=kOutput, calls=%fused_computation.12 | convolution fusion | flops 2533880832 | bytes 21258240 | tf_op jit(solution)/shard_map/dot_general | solution.py:155
  308.2 7.8 convolution_bitcast_fusion
  321.3 11.3 %multiply_bitcast_fusion = f32[4,128,12,64]{1,3,2,0:T(8,128)S(1)} fusion(bf16[4,1024,12,64]{1,3,2,0:T(8,128)(2,1)} %bitcast.165, bf16[4,12,128,1024]{3,2,1,0:T(8,128)(2,1)} %multiply_convert_fusion), kind=kOutput, calls=%fused_computation.82 | convolution fusion | flops 805699584 | bytes 20447232 | tf_op jit(solution)/shard_map/shqk,skhd->sqhd/dot_general | solution.py:176
  340.7 82.4 %reduce-scatter.3.cloned.1.call-done = f32[4,128,1536]{1,2,0:T(8,128)} async-done(((f32[4,1024,1536]{1,2,0:T(8,128)}), f32[4,128,1536]{1,2,0:T(8,128)}) %reduce-scatter.3.cloned.1.call-update) | async-done | bytes 3145744 | tf_op jit(solution)/shard_map/reduce_scatter | solution.py:192
  436.1 19.6 %pad_maximum_fusion = f32[768,9216]{1,0:T(8,128)} fusion(f32[768,3072]{1,0:T(8,128)} %convolution_bitcast_fusion, f32[768,3072]{1,0:T(8,128)} %fusion.86, f32[768,768]{1,0:T(8,128)S(1)} %copy.57, f32[768,2304]{1,0:T(8,128)} %fusion.9), kind=kLoop, calls=%fused_computation | loop fusion | flops 21233664 | bytes 56623104 | tf_op jit(solution)/shard_map/concatenate | solution.py:239
  455.8 173.4 %reduce-scatter.5.cloned.1.call-done = f32[96,9216]{1,0:T(8,128)} async-done(((f32[768,9216]{1,0:T(8,128)}), f32[96,9216]{1,0:T(8,128)}) %reduce-scatter.5.cloned.1.call-update) | async-done | bytes 3538960 | tf_op jit(solution)/shard_map/reduce_scatter | solution.py:238
  630.9 76.9 %collective-permute-done = f32[96,9216]{1,0:T(8,128)} collective-permute-done((f32[96,9216]{1,0:T(8,128)}, f32[96,9216]{1,0:T(8,128)}, u32[]{:S(2)}, u32[]{:S(2)}) %collective-permute-start) | collective-permute-done | bytes 3538976 | tf_op jit(solution)/shard_map/ppermute | solution.py:254
  730.9 157.9 %all-reduce.18 = (f32[768]{0:T(1024)S(1)}, f32[768]{0:T(1024)S(1)}, f32[768]{0:T(1024)S(1)}, f32[768]{0:T(1024)S(1)}, f32[2304]{0:T(1024)S(1)}, /*index=5*/f32[768]{0:T(1024)S(1)}, f32[3072]{0:T(1024)S(1)}) all-reduce(f32[768]{0:T(1024)S(1)} %get-tuple-element.23, ...), channel_id=1, replica_groups=mesh['rep'=4,'fsdp'=8] {'rep','fsdp'}, use_global_device_ids=true, to_apply=%region_12.13 | all-reduce | flops 9216 | bytes 73728 | tf_op jit(solution)/shard_map/psum | solution.py:220
  (199 shorter events, 100.7 us)
Async XLA Ops:
  7.2 42.0 %all-gather.8.cloned.1.call-start = ((), (), s32[]{:S(2)}) async-start(), calls=%async_computation.2 | async-start | bytes 3981312 | tf_op jit(solution)/shard_map/all_gather | solution.py:76
  7.9 69.7 %all-gather.14.cloned.1.call-start = ((), (), s32[]{:S(2)}) async-start(), calls=%async_computation.5 | async-start | bytes 1327104 | tf_op jit(solution)/shard_map/all_gather | solution.py:138
  8.7 113.3 %all-gather.12.cloned.1.call-start = ((), (), s32[]{:S(2)}) async-start(), calls=%async_computation.4 | async-start | bytes 7077888 | tf_op jit(solution)/shard_map/all_gather | solution.py:124
  10.0 45.3 %copy-start.24 = (f32[512]{0:T(512)}, f32[512]{0:T(512)S(1)}, u32[]{:S(2)}) copy-start(f32[512]{0:T(512)S(1)} %get-tuple-element.73) | copy-start | bytes 6148
  11.6 263.9 %copy-start.28 = (f32[4,128]{1,0:T(4,128)}, f32[4,128]{1,0:T(4,128)S(1)}, u32[]{:S(2)}) copy-start(f32[4,128]{1,0:T(4,128)S(1)} %fusion.28) | copy-start | bytes 6148
  12.5 58.2 %copy-start.16 = (f32[4,128,16]{1,2,0:T(8,128)}, f32[4,128,16]{1,2,0:T(8,128)S(1)}, u32[]{:S(2)}) copy-start(f32[4,128,16]{1,2,0:T(8,128)S(1)} %get-tuple-element.67) | copy-start | bytes 98308
  12.5 58.2 %copy-start.18 = (f32[4,128,16]{1,2,0:T(8,128)}, f32[4,128,16]{1,2,0:T(8,128)S(1)}, u32[]{:S(2)}) copy-start(f32[4,128,16]{1,2,0:T(8,128)S(1)} %get-tuple-element.68) | copy-start | bytes 98308
  47.5 228.0 %copy-start.20 = (f32[768]{0:T(1024)}, f32[768]{0:T(1024)S(1)}, u32[]{:S(2)}) copy-start(f32[768]{0:T(1024)S(1)} %convert_element_type.126) | copy-start | bytes 9220
  72.8 98.2 %all-gather.10.cloned.1.call-start = ((), (), s32[]{:S(2)}) async-start(), calls=%async_computation.3 | async-start | bytes 7077888 | tf_op jit(solution)/shard_map/all_gather | solution.py:125
  75.6 201.1 %all-gather.16.cloned.1.call-start = ((), (), s32[]{:S(2)}) async-start(), calls=%async_computation.6 | async-start | bytes 5308416 | tf_op jit(solution)/shard_map/all_gather | solution.py:77
  76.2 209.3 %all-gather.18.cloned.1.call-start = ((), (), s32[]{:S(2)}) async-start(), calls=%async_computation.7 | async-start | bytes 5308416 | tf_op jit(solution)/shard_map/all_gather | solution.py:139
  76.8 346.2 %reduce-scatter.3.cloned.1.call-start = ((), (), s32[]{:S(2)}) async-start(), calls=%async_computation.8 | async-start | bytes 28311552 | tf_op jit(solution)/shard_map/reduce_scatter | solution.py:192
  265.3 363.9 %reduce-scatter.5.cloned.1.call-start = ((), (), s32[]{:S(2)}) async-start(), calls=%async_computation.9 | async-start | bytes 31850496 | tf_op jit(solution)/shard_map/reduce_scatter | solution.py:238
  285.6 19.4 %copy-start.2 = (f32[512,3072]{1,0:T(8,128)S(1)}, f32[512,3072]{1,0:T(8,128)}, u32[]{:S(2)}) copy-start(f32[512,3072]{1,0:T(8,128)} %fusion.83) | copy-start | bytes 18874372
  338.6 86.6 %copy-start.19 = (f32[4,128,16]{1,2,0:T(8,128)S(1)}, f32[4,128,16]{1,2,0:T(8,128)}, u32[]{:S(2)}) copy-start(f32[4,128,16]{1,2,0:T(8,128)} %copy-done.18) | copy-start | bytes 98308
  340.6 85.0 %copy-start.17 = (f32[4,128,16]{1,2,0:T(8,128)S(1)}, f32[4,128,16]{1,2,0:T(8,128)}, u32[]{:S(2)}) copy-start(f32[4,128,16]{1,2,0:T(8,128)} %copy-done.16) | copy-start | bytes 98308
  455.7 174.9 %copy-start.31 = (bf16[768]{0:T(1024)(128)(2,1)S(1)}, bf16[768]{0:T(1024)(128)(2,1)}, u32[]{:S(2)}) copy-start(bf16[768]{0:T(1024)(128)(2,1)} %get-tuple-element.34) | copy-start | bytes 4612
  455.7 174.9 %copy-start.30 = (bf16[768]{0:T(1024)(128)(2,1)S(1)}, bf16[768]{0:T(1024)(128)(2,1)}, u32[]{:S(2)}) copy-start(bf16[768]{0:T(1024)(128)(2,1)} %get-tuple-element.33) | copy-start | bytes 4612
  629.2 78.6 %collective-permute-start = (f32[96,9216]{1,0:T(8,128)}, f32[96,9216]{1,0:T(8,128)}, u32[]{:S(2)}, u32[]{:S(2)}) collective-permute-start(f32[96,9216]{1,0:T(8,128)} %reduce-scatter.5.cloned.1.call-done), channel_id=1, source_target_pairs={{0,8},{8,0},{16,24},{24,16},{1,9},{9,1},{17,25},{25,17},{2,10},{10... | collective-permute-start | bytes 10616840 | tf_op jit(solution)/shard_map/ppermute | solution.py:254
  630.7 84.8 %slice-start.1 = ((s8[4718592]{0:T(1024)(128)(4,1)}), s8[4194304]{0:T(1024)(128)(4,1)S(1)}, s32[]{:S(2)}) async-start(s8[4718592]{0:T(1024)(128)(4,1)} %bitcast.180), calls=%async_computation.11 | async-start | bytes 8388608
  630.8 84.7 %slice-start.2 = ((s8[4718592]{0:T(1024)(128)(4,1)}), s8[524288]{0:T(1024)(128)(4,1)S(1)}, s32[]{:S(2)}) async-start(s8[4718592]{0:T(1024)(128)(4,1)} %bitcast.180), calls=%async_computation.12 | async-start | bytes 1048576
  630.9 84.7 %copy-start.9 = (bf16[512,3072]{1,0:T(8,128)(2,1)S(1)}, bf16[512,3072]{1,0:T(8,128)(2,1)}, u32[]{:S(2)}) copy-start(bf16[512,3072]{1,0:T(8,128)(2,1)} %copy-done.8) | copy-start | bytes 9437188
  713.1 182.5 %collective-permute-start.1 = (f32[96,9216]{1,0:T(8,128)}, f32[96,9216]{1,0:T(8,128)}, u32[]{:S(2)}, u32[]{:S(2)}) collective-permute-start(f32[96,9216]{1,0:T(8,128)} %add.201), channel_id=1, source_target_pairs={{0,16},{8,24},{16,0},{24,8},{1,17},{9,25},{17,1},{25,9},{2,18},{10... | collective-permute-start | bytes 10616840 | tf_op jit(solution)/shard_map/ppermute | solution.py:254
  888.9 13.4 %copy-start.34 = (f32[96]{0:T(128)}, f32[96]{0:T(128)S(1)}, u32[]{:S(2)}) copy-start(f32[96]{0:T(128)S(1)} %dynamic_slice.26) | copy-start | bytes 1156
  (26 other events, 116.8 us)
Sparse Core Ops, SparseCore 0:
  9.9 36.8 all-gather.7
  48.7 24.0 all-gather.13
  75.2 46.6 all-gather.11
  124.2 46.6 all-gather.9
  172.7 38.9 all-gather.15
  213.4 38.9 all-gather.17
  265.4 157.5 reduce-scatter.2
  455.9 173.2 reduce-scatter.4
